TPU v7x, 128 devices: a whole 4x4x4 slice. The times are simulated.
128 devices in a mesh: grp: 4 (over x_hi, core), dev: 32 (over x_lo, y, z).
Axes of the slice: x: 4 (x_hi: 2, x_lo: 2; x = x_hi * 2 + x_lo), y: 4, z: 4, core: 2. Of those that a mesh axis runs over, the one named last changes fastest.
Arguments:
- projections: float32 [24576, 1024], P(('grp', 'dev')), as said below
- row_weights: bfloat16 [24576], P(('grp', 'dev')), may hold values from 0.5 to 2
- partner: int32 [24576], P(('grp', 'dev')), may hold values from 0 to 24575, as said below
Outputs:
- losses: float32 [24576], P(('grp', 'dev'))
- gradient: float32 [24576, 1024], P(('grp', 'dev'))
Inputs may be any that keep to these rules, and one draw needn't show every extreme that they name: partner[partner[i]] = i and partner[i] != i for every view i: the views come in pairs, two to an image. `projections`: every row is nonzero.
All inputs are finite; a program needn't handle non-finite values.
Results may differ from a plain program's by a relative error of at most 0.0052.
Values may be sent and summed in bfloat16 or wider, within the bound.
A program may use at most 128 MiB of HBM per device.

v0:
```python
import math

import jax
import jax.numpy as jnp
from jax import lax
from jax.sharding import PartitionSpec as P

inv_temp = 10.0
epsilon = 1e-06


def score_tile(row_views, col_views):
    return (
        lax.dot_general(
            row_views, col_views, (((1,), (1,)), ((), ())), preferred_element_type=jnp.float32
        )
        * inv_temp
    )


def local(projections, row_weights, partner):
    rows_dev, feat_width = projections.shape
    dev_count = lax.axis_size("dev")
    grp_count = lax.axis_size("grp")
    grp_at = lax.axis_index("grp")
    dev_at = lax.axis_index("dev")
    inv_norm = lax.rsqrt(jnp.sum(projections * projections, axis=1, keepdims=True) + epsilon)
    unit = projections * inv_norm
    views = unit.astype(jnp.bfloat16)
    group_views, group_weights = (
        lax.all_gather(views, "dev", axis=0, tiled=True),
        lax.all_gather(row_weights, "dev", axis=0, tiled=True),
    )
    cross_views, cross_weights = (
        lax.all_gather(views, "grp", axis=0, tiled=True),
        lax.all_gather(row_weights, "grp", axis=0, tiled=True),
    )
    group_partner = lax.all_gather(partner, "dev", axis=0, tiled=True)
    group_len = dev_count * rows_dev
    group_base = grp_at * group_len
    cross_ids = (
        (jnp.arange(grp_count, dtype=jnp.int32)[:, None] * dev_count + dev_at) * rows_dev
        + jnp.arange(rows_dev, dtype=jnp.int32)[None, :]
    ).reshape(-1)
    cross_w = cross_weights.astype(jnp.float32)
    group_w = group_weights.astype(jnp.float32)
    shards = min(dev_count, max(1, -(-512 // rows_dev)))
    while dev_count % shards:
        shards += 1
    block_rows = shards * rows_dev
    block_count = group_len // block_rows

    def tile_parts(row_start, row_count):
        row_views = lax.dynamic_slice_in_dim(group_views, row_start, row_count, 0)
        scores = score_tile(row_views, cross_views)
        row_ids = group_base + row_start + jnp.arange(row_count, dtype=jnp.int32)
        on_diag = row_ids[:, None] == cross_ids[None, :]
        partner_rows = lax.dynamic_slice_in_dim(group_partner, row_start, row_count, 0)
        is_partner = partner_rows[:, None] == cross_ids[None, :]
        return (row_views, scores, on_diag, is_partner)

    def row_stats(block_at):
        row_views, scores, on_diag, is_partner = tile_parts(block_at * block_rows, block_rows)
        terms = jnp.where(on_diag, 0.0, jnp.exp(scores - inv_temp))
        return (jnp.sum(terms, axis=1), jnp.sum(jnp.where(is_partner, scores, 0.0), axis=1))

    exp_sums, positive = lax.map(row_stats, jnp.arange(block_count, dtype=jnp.int32))
    exp_sums, positive = (
        lax.psum_scatter(exp_sums.reshape(-1), "dev", scatter_dimension=0, tiled=True),
        lax.psum_scatter(positive.reshape(-1), "dev", scatter_dimension=0, tiled=True),
    )
    own_lse = inv_temp + jnp.log(exp_sums)
    losses = own_lse - positive
    every_lse = lax.all_gather(own_lse, ("grp", "dev"), axis=0, tiled=True)
    group_lse = lax.dynamic_slice_in_dim(every_lse, group_base, group_len, 0)
    cross_lse = lax.dynamic_slice_in_dim(
        every_lse.reshape(grp_count, group_len), dev_at * rows_dev, rows_dev, 1
    ).reshape(-1)

    def coupling(row_start, row_count):
        row_views, scores, on_diag, is_partner = tile_parts(row_start, row_count)
        row_lse = lax.dynamic_slice_in_dim(group_lse, row_start, row_count, 0)
        row_w = lax.dynamic_slice_in_dim(group_w, row_start, row_count, 0)
        toward = jnp.exp(scores - row_lse[:, None])
        reverse_p = jnp.exp(scores - cross_lse[None, :])
        coupled = row_w[:, None] * toward + cross_w[None, :] * reverse_p
        coupled = coupled - (row_w[:, None] + cross_w[None, :]) * jnp.where(is_partner, 1.0, 0.0)
        return (row_views, jnp.where(on_diag, 0.0, coupled).astype(jnp.bfloat16))

    row_count = rows_dev * lax.axis_size("dev")
    piece_rows = math.gcd(row_count, block_rows)
    piece_count = row_count // piece_rows

    def piece_term(piece_at):
        row_views, weights_tile = coupling(piece_at * piece_rows, piece_rows)
        return jnp.dot(weights_tile, cross_views, preferred_element_type=jnp.float32) * inv_temp

    dview = lax.psum_scatter(
        lax.map(piece_term, jnp.arange(piece_count, dtype=jnp.int32)).reshape(
            row_count, feat_width
        ),
        "dev",
        scatter_dimension=0,
        tiled=True,
    )
    gradient = inv_norm * (dview - unit * jnp.sum(unit * dview, axis=1, keepdims=True))
    return (losses, gradient)


def solution(mesh):
    return jax.shard_map(
        local,
        mesh=mesh,
        in_specs=(P(("grp", "dev"), None), P(("grp", "dev")), P(("grp", "dev"))),
        out_specs=(P(("grp", "dev")), P(("grp", "dev"), None)),
        check_vma=False,
    )
```

profile of v0, /device:TPU:0, one launch (start us, length us, event | category | flops | bytes accessed | tf_op | source)
XLA Modules:
  0.0 939.6 jit_solution(5261191398424124840)
XLA Ops:
  13.5 159.8 %all-reduce = s32[6144]{0:T(1024)S(1)} all-reduce(s32[6144]{0:T(1024)S(1)} %dynamic-update-slice), channel_id=1, replica_groups=mesh['grp'=4,'dev'=32] {'dev'}, use_global_device_ids=true, to_apply=%add | all-reduce | flops 6144 | bytes 49152
  173.3 42.7 %all-gather.3.cloned.1.call-done = bf16[6144,1024]{1,0:T(8,128)(2,1)} async-done(((bf16[192,1024]{1,0:T(8,128)(2,1)}), bf16[6144,1024]{1,0:T(8,128)(2,1)}) %all-gather.3.cloned.1.call-update) | async-done | bytes 12582928 | tf_op jit(solution)/shard_map/all_gather | solution.py:31
  216.0 43.1 %while.27 = (s32[]{:T(128)}, f32[8,768]{1,0:T(8,128)S(1)}, f32[8,768]{1,0:T(8,128)S(1)}, s32[8]{0:T(128)S(1)}, s32[]{:T(128)}, /*index=5*/bf16[6144,1024]{1,0:T(...) while((s32[]{:T(128)}, f32[8,768]{1,0:T(8,128)S(1)}, ...), condition=%wide.region_4.5_spmd.clone, body=%wide.region_1.4_spmd.clone.sunk | while | flops 1212678144 | bytes 3204327 | solution.py:67
  217.5 3.7 select_reduce_fusion.3
  222.9 3.7 select_reduce_fusion.3
  228.3 3.7 select_reduce_fusion.3
  233.7 3.7 select_reduce_fusion.3
  239.1 3.7 select_reduce_fusion.3
  244.5 3.7 select_reduce_fusion.3
  249.8 3.7 select_reduce_fusion.3
  255.2 3.7 select_reduce_fusion.3
  259.2 155.0 %all-reduce.6 = (f32[6144]{0:T(1024)S(1)}, f32[6144]{0:T(1024)S(1)}) all-reduce(f32[6144]{0:T(1024)S(1)} %reshape.53, f32[6144]{0:T(1024)S(1)} %reshape.52), channel_id=3, replica_groups=mesh['grp'=4,'dev'=32] {'dev'}, use_global_device_ids=true, to_apply=%region_6.7.clone | all-reduce | flops 12288 | bytes 98304
  416.0 152.1 %all-reduce.1 = bf16[6144]{0:T(1024)(128)(2,1)S(1)} all-reduce(bf16[6144]{0:T(1024)(128)(2,1)S(1)} %dynamic-update-slice.1), channel_id=1, replica_groups=mesh['grp'=4,'dev'=32] {'dev'}, use_global_device_ids=true, to_apply=%add.1 | all-reduce | flops 6144 | bytes 24576
  569.6 7.1 all-reduce.3
  578.6 77.5 %while.28 = (s32[]{:T(128)}, f32[8,768,1024]{2,1,0:T(8,128)}, s32[8]{0:T(128)S(1)}, s32[]{:T(128)}, f32[6144]{0:T(1024)S(1)}, /*index=5*/bf16[6144,1024]{1,0:T(8...) while((s32[]{:T(128)}, f32[8,768,1024]{2,1,0:T(8,128)}, ...), condition=%wide.wide.region_8.9_spmd.clone, body=%wide.wide.region_7.8_spmd.clone.sunk | while | flops 2424964608 | bytes 7917319 | solution.py:99
  580.2 8.0 bitcast_dynamic-update-slice_fusion.3
  589.9 8.1 bitcast_dynamic-update-slice_fusion.3
  599.6 8.1 bitcast_dynamic-update-slice_fusion.3
  609.3 8.0 bitcast_dynamic-update-slice_fusion.3
  619.0 8.0 bitcast_dynamic-update-slice_fusion.3
  628.7 8.0 bitcast_dynamic-update-slice_fusion.3
  638.4 8.1 bitcast_dynamic-update-slice_fusion.3
  648.1 8.0 bitcast_dynamic-update-slice_fusion.3
  656.1 273.3 %reduce-scatter.2.cloned.1.call-done = f32[192,1024]{1,0:T(8,128)} async-done(((f32[6144,1024]{1,0:T(8,128)}), f32[192,1024]{1,0:T(8,128)}) %reduce-scatter.2.cloned.1.call-update) | async-done | bytes 786448 | tf_op jit(solution)/shard_map/reduce_scatter | solution.py:98
  (181 shorter events, 29.0 us)
Async XLA Ops:
  7.2 4.2 copy-start.3
  7.2 6.1 copy-start.4
  7.2 166.1 %all-gather.5.cloned.1.call-start = ((), (), s32[]{:S(2)}) async-start(), calls=%async_computation.2 | async-start | bytes 1966080 | tf_op jit(solution)/shard_map/all_gather | solution.py:35
  10.5 205.5 %all-gather.3.cloned.1.call-start = ((), (), s32[]{:S(2)}) async-start(), calls=%async_computation.1 | async-start | bytes 12976128 | tf_op jit(solution)/shard_map/all_gather | solution.py:31
  11.3 565.4 %all-reduce.9.cloned.1.call-start = ((), (), s32[]{:S(2)}) async-start(), calls=%async_computation.4 | async-start | bytes 196608
  216.0 199.7 %copy-start.5 = (bf16[192]{0:T(256)(128)(2,1)S(1)}, bf16[192]{0:T(256)(128)(2,1)}, u32[]{:S(2)}) copy-start(bf16[192]{0:T(256)(128)(2,1)} %param.8) | copy-start | bytes 1156
  216.0 352.1 %copy-start.6 = (u32[128]{0:T(128)S(1)}, u32[128]{0:T(128)}, u32[]{:S(2)}) copy-start(u32[128]{0:T(128)} %constant.109) | copy-start | bytes 1540
  415.0 0.6 copy-start.1
  415.6 513.8 %reduce-scatter.2.cloned.1.call-start = ((), (), s32[]{:S(2)}) async-start(), calls=%async_computation.3 | async-start | bytes 25952256 | tf_op jit(solution)/shard_map/reduce_scatter | solution.py:98
  577.7 0.8 copy-start.2
  656.1 273.4 %copy-start = (f32[192,1024]{1,0:T(8,128)S(1)}, f32[192,1024]{1,0:T(8,128)}, u32[]{:S(2)}) copy-start(f32[192,1024]{1,0:T(8,128)} %param.7) | copy-start | bytes 2359300
Sparse Core Ops, SparseCore 0:
  10.6 26.2 all-gather.4
  39.2 176.8 all-gather.2
  415.7 133.3 all-reduce.8
  656.2 273.1 reduce-scatter.1
where the time goes:
time: 941 us; the launch traced here: 940 us
  blocking collectives  474 us (50%)
  waiting for transfers between devices  317 us (34%)
  matrix products  93.8 us (10%)
  local copies, waits for them, and re-layouts  19.3 us (2%)
  between operations  15.8 us (2%)
  loops' own time  10.9 us (1%)
    unnamed x4, blocking collectives  474 us
    reduce_scatter x1, waiting for transfers between devices, local(): lax.psum_scatter(lax.map(piece_term, jnp.arange(piece_count, dtype=jnp.in...  273 us
    dot_general x8, matrix products, piece_term(): jnp.dot(weights_tile, cross_views, preferred_element_type=jnp.float32)  64.3 us
    all_gather x1, waiting for transfers between devices, local(): lax.all_gather(views, 'dev', axis=0, tiled=True)  42.7 us
    dot_general x8, matrix products, score_tile(): lax.dot_general(row_views, col_views, (((1,), (1,)), ((), ())), preferred...  29.4 us
  transfers between devices with their start and end apart: 4, of which 2 were waited for; matrix products, arithmetic and copies ran while one was open for 0% of the time, Pallas kernels for 0%

commit v1 on v0

v1 whole, which is shorter than its diff:
```python
import jax
import jax.numpy as jnp
from jax import lax
from jax.experimental import pallas as pl
from jax.experimental.pallas import tpu as pltpu
from jax.sharding import PartitionSpec as P

MESH = pl.DeviceIdType.MESH
inv_temp = 10.0
epsilon = 1e-06

SLOTS = (
    (2, 0, 1), (0, 2, 3), (1, 3, 3), (1, 2, 0), (3, 0, 1), (0, 0, 1),
    (0, 0, 3), (0, 3, 3), (1, 1, 0), (3, 0, 0), (0, 0, 0),
)
PARENT = (4, 7, 7, 8, 9, 10, 10, 10, 10, 10)
KIDS = ((0, 0), (0, 0), (0, 0), (0, 0), (0, 1), (0, 0), (0, 0), (1, 3), (3, 4), (4, 5), (5, 10))
SELF = 10
COUNT = 11
STEPS = (
    ((7, 10, 2, 8, 2), (9, 7, 2, 8, 2), (4, 7, 2, 6, 2), (10, 10, 2, 6, 2), (7, 5, 2, 1, 2),
     (9, 6, 2, 3, 1), (5, 8, 2, 1, 1), (2, 8, 2, 3, 2), (0, 5, 1, 6, 1)),
    ((10, 9, 2, 8, 2), (6, 8, 2, 5, 1), (2, 4, 2, 6, 2), (9, 5, 2, 2, 2), (4, 8, 2, 1, 2),
     (1, 9, 2, 6, 1), (3, 10, 2, 4, 2), (0, 10, 2, 8, 2), (0, 1, 1, 2, 2)),
)
NSTEP = 9
ZERO = 2 * NSTEP
CHUNKS = 3
RB = 32

NT = (((1,), (1,)), ((), ()))
NN = (((1,), (0,)), ((), ()))
TN = (((0,), (0,)), ((), ()))


def diff(a, b):
    return tuple((x - y) % 4 for x, y in zip(a, b))


def neg(a):
    return tuple(-x % 4 for x in a)


EDGE = tuple(diff(SLOTS[k], SLOTS[PARENT[k]]) for k in range(COUNT - 1))
PARTNERS = sorted(
    {d for s in SLOTS[:SELF] + EDGE for d in (s, neg(s))}
)


def backward_plan():
    out = []
    for steps in STEPS:
        prep, rows, cols, cols_a = [], [], [], []
        pb, rb, cb = [0], [0], [0]
        for k in range(COUNT):
            mine = []
            for t, (a, b1, _, b2, _) in enumerate(steps):
                if k in (a, b1, b2) and t not in prep:
                    prep.append(t)
                if a == k:
                    rows.append(t)
                for u, b in ((0, b1), (1, b2)):
                    if b == k and a != b:
                        mine.append((2 * t + u, a))
            if len(mine) % 2:
                mine.append((ZERO, SELF))
            for i in range(0, len(mine), 2):
                cols.append((mine[i][0], mine[i + 1][0], mine[i][1], mine[i + 1][1]))
            pb.append(len(prep))
            rb.append(len(rows))
            cb.append(len(cols))
        out.append((prep, rows, cols, pb, rb, cb))
    return out


PLAN = backward_plan()

UP_AFTER = (
    (), ((0, 0), (0, 1), (0, 2)), ((1, 0), (1, 1), (1, 2)), ((2, 0), (2, 1), (2, 2)),
    ((3, 0), (3, 1), (3, 2)), ((4, 0),), ((5, 0), (5, 1), (5, 2), (4, 1)),
    ((6, 0), (6, 1), (6, 2), (4, 2)), ((7, 0), (8, 0)), ((9, 0), (7, 1), (8, 1)),
    ((7, 2), (8, 2), (9, 1), (9, 2)),
)
UPS = tuple(e for l in UP_AFTER for e in l)
UP_BOUND = tuple(sum(len(l) for l in UP_AFTER[:i]) for i in range(COUNT + 1))


def lut(i, table):
    v = jnp.int32(table[0])
    for n in range(1, len(table)):
        v = jnp.where(i == n, jnp.int32(table[n]), v)
    return v


def lut2(i, c, t0, t1):
    n = max(len(t0), len(t1))
    t0 = tuple(t0) + (0,) * (n - len(t0))
    t1 = tuple(t1) + (0,) * (n - len(t1))
    if t0 == t1:
        return lut(i, t0)
    return lut(i, t0) * (1 - c) + lut(i, t1) * c


def kernel(
    x_ref, xw_ref, loss_ref, grad_ref,
    V, XT, XB, E, C, S, acc, H, TX, RX, RC, rsum, rpos, csum, cpos, SO, SI, SR, AO, AR, acol, wcol,
    gs, gr, ss, sr, us, ur, ts, tr, ms, mr, ps, pr, qs, qr,
):
    rows, width = x_ref.shape
    block = 2 * rows
    part = rows // CHUNKS
    grp = lax.axis_index("grp")
    dev = lax.axis_index("dev")
    c = grp % 2
    px, py, pz = (grp // 2) * 2 + dev // 16, (dev // 4) % 4, dev % 4

    def device(d, core):
        x, y, z = (px + d[0]) % 4, (py + d[1]) % 4, (pz + d[2]) % 4
        return ((x // 2) * 2 + core, (x % 2) * 16 + y * 4 + z)

    sibling = device((0, 0, 0), 1 - c)

    barrier = pltpu.get_barrier_semaphore()
    for d in PARTNERS:
        pl.semaphore_signal(barrier, inc=1, device_id=device(d, c), device_id_type=MESH)
    pl.semaphore_signal(barrier, inc=1, device_id=sibling, device_id_type=MESH)

    def base_of(k):
        x = (px + lut(k, [d[0] for d in SLOTS])) % 4
        y = (py + lut(k, [d[1] for d in SLOTS])) % 4
        z = (pz + lut(k, [d[2] for d in SLOTS])) % 4
        return ((x // 2) * 64 + (x % 2) * 16 + y * 4 + z) * rows

    own = pl.multiple_of(c * rows, 64)
    other = pl.multiple_of((1 - c) * rows, 64)

    def norm_body(i, _):
        r = pl.multiple_of(i * 32, 32)
        x = x_ref[pl.ds(r, 32), :]
        inv = lax.rsqrt(jnp.sum(x * x, axis=1, keepdims=True) + epsilon)
        V[SELF, pl.ds(pl.multiple_of(own + r, 32), 32), :] = (x * inv).astype(jnp.bfloat16)
        return 0

    lax.fori_loop(0, rows // 32, norm_body, 0)
    XT[SELF, c] = xw_ref[...]
    for ref in (rsum, rpos, csum, cpos):
        ref[...] = jnp.zeros_like(ref)

    pl.semaphore_wait(barrier, len(PARTNERS) + 1)

    def piece(k, j, core):
        if j == CHUNKS:
            return XT.at[k, core]
        r = pl.multiple_of(core * rows + j * part, 64)
        return V.at[k, pl.ds(r, part), :]

    def tree_copy(k, j):
        src, dst = piece(PARENT[k], j, c), piece(k, j, c)
        return pltpu.make_async_remote_copy(
            src_ref=src, dst_ref=dst, send_sem=gs.at[k, j], recv_sem=gr.at[k, j],
            device_id=device(neg(EDGE[k]), c), device_id_type=MESH,
        )

    def twin_copy(k, j):
        ref = piece(k, j, c)
        return pltpu.make_async_remote_copy(
            src_ref=ref, dst_ref=ref, send_sem=ss.at[k, j], recv_sem=sr.at[k, j],
            device_id=sibling, device_id_type=MESH,
        )

    def arrive(k, j):
        tree_copy(k, j).wait_recv()
        for child in range(*KIDS[k]):
            tree_copy(child, j).start()
        twin_copy(k, j).start()

    def twins(k):
        for j in range(CHUNKS + 1):
            twin_copy(k, j).wait_recv()
        XB[k] = XT[k, 0] + XT[k, 1]

    for k in (9, 8, 7, 6, 5):
        tree_copy(k, CHUNKS).start()
    for j in range(CHUNKS):
        for k in (9, 8, 7):
            tree_copy(k, j).start()
        if j == 0:
            tree_copy(5, 0).start()
    for j in range(CHUNKS + 1):
        twin_copy(SELF, j).start()

    def gate0():
        for k in (9, 8, 7):
            arrive(k, CHUNKS)
        for j in range(CHUNKS):
            arrive(9, j)
            if j + 1 < CHUNKS:
                tree_copy(5, j + 1).start()
            arrive(8, j)
            arrive(7, j)
            tree_copy(6, j).start()
        for k in (SELF, 9, 8, 7):
            twins(k)

    def gate1():
        for k in (5, 6, 4):
            arrive(k, CHUNKS)
        for j in range(CHUNKS):
            arrive(4, j)
            arrive(5, j)
        for j in range(CHUNKS):
            arrive(6, j)
        for k in (5, 4, 6):
            twins(k)

    def gate2():
        for k in (3, 2, 1):
            arrive(k, CHUNKS)
        for j in range(CHUNKS):
            for k in (3, 2, 1):
                arrive(k, j)
        for k in (3, 2, 1):
            twins(k)

    def gate3():
        for j in (CHUNKS,) + tuple(range(CHUNKS)):
            arrive(0, j)
        twins(0)

    def step_of(t):
        cols = [[[s[n] for s in STEPS[core]] for n in range(5)] for core in (0, 1)]
        a, b1, h1, b2, h2 = (lut2(t, c, cols[0][n], cols[1][n]) for n in range(5))
        return a, b1, h1.astype(jnp.float32) * 0.5, b2, h2.astype(jnp.float32) * 0.5

    lane = lax.broadcasted_iota(jnp.int32, (1, block), 1)
    sub_row = lax.broadcasted_iota(jnp.int32, (RB, 1), 0)
    far = 32 * rows - rows

    def tile_rows(t):
        a, b1, h1, b2, h2 = step_of(t)
        partner = jnp.concatenate([XB[b1, 1:2, :], XB[b2, 1:2, :]], axis=1)
        weight = jnp.concatenate(
            [jnp.full((1, block), h1, jnp.float32), jnp.full((1, block), h2, jnp.float32)], axis=1
        )
        return a, b1, b2, partner, weight

    def row_ids(a, r):
        start = base_of(a) + r + jnp.where(r >= rows, far, 0)
        return (start + sub_row).astype(jnp.float32)

    def column_ids(b):
        return (base_of(b) + lane + jnp.where(lane >= rows, far, 0)).astype(jnp.float32)

    def score_step(t, _):
        for n, gate in ((0, gate0), (1, gate1), (2, gate2), (7, gate3)):
            pl.when(t == n)(gate)
        a, b1, b2, partner, weight = tile_rows(t)
        S[...] = lax.dot_general(
            V[a], jnp.concatenate([V[b1], V[b2]], axis=0), NT, preferred_element_type=jnp.float32
        )
        ids = jnp.concatenate([column_ids(b1), column_ids(b2)], axis=1)

        def rows_body(i, carry):
            es, ps_ = carry
            r = pl.multiple_of(i * RB, RB)
            s = S[pl.ds(r, RB), :] * inv_temp
            rid = row_ids(a, r)
            e = jnp.exp(s - inv_temp) * weight
            e = jnp.where(rid == ids, 0.0, e)
            m = jnp.where(rid == partner, s * weight, 0.0)
            E[t, pl.ds(r, RB), :] = e
            er, mr_ = e[:, :128], m[:, :128]
            for n in range(1, 2 * block // 128):
                er = er + e[:, n * 128 : (n + 1) * 128]
                mr_ = mr_ + m[:, n * 128 : (n + 1) * 128]
            rsum[a, pl.ds(r, RB), :] += er
            rpos[a, pl.ds(r, RB), :] += mr_
            for n in range(RB // 8):
                es = es + e[n * 8 : (n + 1) * 8, :]
                ps_ = ps_ + m[n * 8 : (n + 1) * 8, :]
            return es, ps_

        zero = jnp.zeros((8, 2 * block), jnp.float32)
        es, ps_ = lax.fori_loop(0, block // RB, rows_body, (zero, zero))
        for n, b in ((0, b1), (1, b2)):
            use = jnp.where(a == b, 0.0, 1.0)
            csum[b] += es[:, n * block : (n + 1) * block] * use
            cpos[b] += ps_[:, n * block : (n + 1) * block] * use
        return 0

    lax.fori_loop(0, NSTEP, score_step, 0)

    def total(rs, cs):
        return jnp.sum(rs.T, axis=0, keepdims=True) + jnp.sum(cs, axis=0, keepdims=True)

    def sums_body(k, _):
        SO[k, 0:1, :] = total(rsum[k], csum[k])
        SO[k, 1:2, :] = total(rpos[k], cpos[k])
        return 0

    SO[...] = jnp.zeros_like(SO)
    lax.fori_loop(0, COUNT, sums_body, 0)

    twin_sums = pltpu.make_async_remote_copy(
        src_ref=SO, dst_ref=SI, send_sem=ms, recv_sem=mr, device_id=sibling, device_id_type=MESH
    )
    twin_sums.start()

    def wide(row):
        return jnp.broadcast_to(row, (128, block)).T

    def wcol_body(k, _):
        wcol[k] = wide(XB[k, 0:1, :])
        return 0

    lax.fori_loop(0, COUNT, wcol_body, 0)
    twin_sums.wait()
    SI[...] = SO[...] + SI[...]

    def sum_copy(k):
        return pltpu.make_async_remote_copy(
            src_ref=SI.at[k], dst_ref=SR.at[k], send_sem=ps.at[k], recv_sem=pr.at[k],
            device_id=device(SLOTS[k], c), device_id_type=MESH,
        )

    def scale_copy(k):
        return pltpu.make_async_remote_copy(
            src_ref=AO, dst_ref=AR.at[k], send_sem=qs.at[k], recv_sem=qr.at[k],
            device_id=device(neg(SLOTS[k]), c), device_id_type=MESH,
        )

    for k in range(COUNT - 1):
        sum_copy(k).start()
    both = SI[SELF]
    for k in range(COUNT - 1):
        sum_copy(k).wait_recv()
        both = both + SR[k]
    exp_sum, positive = both[0:1, :], both[1:2, :]
    scale = XB[SELF, 0:1, :] / exp_sum
    AO[...] = jnp.broadcast_to(scale, (8, block))
    for k in range(COUNT - 1):
        scale_copy(k).start()
    AR[SELF] = AO[...]
    losses = jnp.broadcast_to(inv_temp + jnp.log(exp_sum) - positive, (8, block))
    loss_ref[...] = jnp.where(c == 0, losses, pltpu.roll(losses, rows, 1))
    C[ZERO] = jnp.zeros((block, block), jnp.bfloat16)
    for k in range(COUNT - 1):
        scale_copy(k).wait_recv()

    def acol_body(k, _):
        acol[k] = wide(AR[k, 0:1, :])
        return 0

    lax.fori_loop(0, COUNT, acol_body, 0)

    def twin_part(k):
        return pltpu.make_async_remote_copy(
            src_ref=TX.at[k], dst_ref=RX.at[k], send_sem=ts.at[k], recv_sem=tr.at[k],
            device_id=sibling, device_id_type=MESH,
        )

    def up_copy(k, j, d):
        r = pl.multiple_of(j * part, 64)
        return pltpu.make_async_remote_copy(
            src_ref=TX.at[k, pl.ds(r, part), :], dst_ref=RC.at[k, pl.ds(r, part), :],
            send_sem=us.at[k, j], recv_sem=ur.at[k, j], device_id=device(d, c), device_id_type=MESH,
        )

    def edge_of(k):
        return tuple(lut(k, [e[n] for e in EDGE]) for n in range(3))

    def gathered(k, j, lo, hi):
        r = pl.multiple_of(j * part, 64)

        def child(n, _):
            up_copy(n, j, (0, 0, 1)).wait_recv()
            H[k, pl.ds(r, part), :] += RC[n, pl.ds(r, part), :].astype(jnp.float32)
            return 0

        lax.fori_loop(lo, hi, child, 0)

    def up_event(ev, _):
        k = lut(ev, [e[0] for e in UPS])
        j = lut(ev, [e[1] for e in UPS])

        @pl.when(j == 0)
        def _():
            twin_part(k).wait()

        gathered(k, j, lut(k, [a for a, _ in KIDS]), lut(k, [b for _, b in KIDS]))
        r = pl.multiple_of(j * part, 64)
        TX[k, pl.ds(r, part), :] = (
            H[k, pl.ds(r, part), :] + RX[k, pl.ds(r, part), :].astype(jnp.float32)
        ).astype(jnp.bfloat16)
        up_copy(k, j, edge_of(k)).start()
        return 0

    def prepare(n, _):
        t = lut2(n, c, PLAN[0][0], PLAN[1][0])
        a, b1, b2, partner, weight = tile_rows(t)
        arow = jnp.concatenate([AR[b1, 0:1, :], AR[b2, 0:1, :]], axis=1)
        wrow = jnp.concatenate([XB[b1, 0:1, :], XB[b2, 0:1, :]], axis=1)

        def rows_body(i, _):
            r = pl.multiple_of(i * RB, RB)
            rid = row_ids(a, r)
            ac, wc = acol[a, pl.ds(r, RB), :], wcol[a, pl.ds(r, RB), :]
            ac = jnp.concatenate([ac] * (2 * block // 128), axis=1)
            wc = jnp.concatenate([wc] * (2 * block // 128), axis=1)
            v = E[t, pl.ds(r, RB), :] * (ac + arow)
            v = (v - jnp.where(rid == partner, (wc + wrow) * weight, 0.0)).astype(jnp.bfloat16)
            C[2 * t, pl.ds(r, RB), :] = v[:, :block]
            C[2 * t + 1, pl.ds(r, RB), :] = v[:, block:]
            return 0

        lax.fori_loop(0, block // RB, rows_body, 0)
        return 0

    def row_product(n, _):
        t = lut2(n, c, PLAN[0][1], PLAN[1][1])
        _, b1, _, b2, _ = step_of(t)
        acc[...] += lax.dot_general(
            jnp.concatenate([C[2 * t], C[2 * t + 1]], axis=1),
            jnp.concatenate([V[b1], V[b2]], axis=0),
            NN, preferred_element_type=jnp.float32,
        )
        return 0

    def column_product(n, _):
        u1, u2, a1, a2 = (
            lut2(n, c, [q[i] for q in PLAN[0][2]], [q[i] for q in PLAN[1][2]]) for i in range(4)
        )
        acc[...] += lax.dot_general(
            jnp.concatenate([C[u1], C[u2]], axis=0),
            jnp.concatenate([V[a1], V[a2]], axis=0),
            TN, preferred_element_type=jnp.float32,
        )
        return 0

    def slot_body(k, _):
        for n, body in ((3, prepare), (4, row_product), (5, column_product)):
            if n == 4:
                acc[...] = jnp.zeros_like(acc)
            lo = lut2(k, c, PLAN[0][n][:-1], PLAN[1][n][:-1])
            hi = lut2(k, c, PLAN[0][n][1:], PLAN[1][n][1:])
            lax.fori_loop(lo, hi, body, 0)
        H[k] = acc[pl.ds(own, rows), :]
        TX[k] = acc[pl.ds(other, rows), :].astype(jnp.bfloat16)
        twin_part(k).start()
        lax.fori_loop(lut(k, UP_BOUND[:-1]), lut(k, UP_BOUND[1:]), up_event, 0)
        return 0

    lax.fori_loop(0, COUNT, slot_body, 0)

    twin_part(SELF).wait()

    def finish(j, _):
        gathered(SELF, j, *KIDS[SELF])

        def body(i, _):
            r = pl.multiple_of(j * part + i * 16, 16)
            x = x_ref[pl.ds(r, 16), :]
            inv = lax.rsqrt(jnp.sum(x * x, axis=1, keepdims=True) + epsilon)
            unit = x * inv
            dview = (H[SELF, pl.ds(r, 16), :] + RX[SELF, pl.ds(r, 16), :].astype(jnp.float32)) * inv_temp
            grad_ref[pl.ds(r, 16), :] = inv * (
                dview - unit * jnp.sum(unit * dview, axis=1, keepdims=True)
            )
            return 0

        lax.fori_loop(0, part // 16, body, 0)
        return 0

    lax.fori_loop(0, CHUNKS, finish, 0)

    for k in range(COUNT - 1):
        for j in range(CHUNKS + 1):
            tree_copy(k, j).wait_send()
        for j in range(CHUNKS):
            up_copy(k, j, EDGE[k]).wait_send()
        sum_copy(k).wait_send()
        scale_copy(k).wait_send()
    for k in range(COUNT):
        for j in range(CHUNKS + 1):
            twin_copy(k, j).wait_send()


def local(projections, row_weights, partner):
    rows, width = projections.shape
    block = 2 * rows
    core = lax.axis_index("grp") % 2
    mine = jnp.stack([row_weights.astype(jnp.float32), partner.astype(jnp.float32)])
    mine = jnp.pad(mine, ((0, 6), (0, 0)))
    none = jnp.zeros_like(mine)
    extras = jnp.where(
        core == 0, jnp.concatenate([mine, none], 1), jnp.concatenate([none, mine], 1)
    )
    f32, bf16 = jnp.float32, jnp.bfloat16
    vm, dma = pltpu.VMEM, pltpu.SemaphoreType.DMA
    losses, gradient = pl.pallas_call(
        kernel,
        out_shape=(
            jax.ShapeDtypeStruct((8, block), f32),
            jax.ShapeDtypeStruct((rows, width), f32),
        ),
        in_specs=[pl.BlockSpec(memory_space=vm)] * 2,
        out_specs=[pl.BlockSpec(memory_space=vm)] * 2,
        scratch_shapes=[
            vm((COUNT, block, width), bf16),
            vm((COUNT, 2, 8, block), f32),
            vm((COUNT, 8, block), f32),
            vm((NSTEP, block, 2 * block), f32),
            vm((2 * NSTEP + 1, block, block), bf16),
            vm((block, 2 * block), f32),
            vm((block, width), f32),
            vm((COUNT, rows, width), f32),
            vm((COUNT, rows, width), bf16),
            vm((COUNT, rows, width), bf16),
            vm((COUNT - 1, rows, width), bf16),
            vm((COUNT, block, 128), f32),
            vm((COUNT, block, 128), f32),
            vm((COUNT, 8, block), f32),
            vm((COUNT, 8, block), f32),
            vm((COUNT, 8, block), f32),
            vm((COUNT, 8, block), f32),
            vm((COUNT - 1, 8, block), f32),
            vm((8, block), f32),
            vm((COUNT, 8, block), f32),
            vm((COUNT, block, 128), f32),
            vm((COUNT, block, 128), f32),
            dma((COUNT - 1, CHUNKS + 1)), dma((COUNT - 1, CHUNKS + 1)),
            dma((COUNT, CHUNKS + 1)), dma((COUNT, CHUNKS + 1)),
            dma((COUNT - 1, CHUNKS)), dma((COUNT - 1, CHUNKS)),
            dma((COUNT,)), dma((COUNT,)),
            dma, dma,
            dma((COUNT - 1,)), dma((COUNT - 1,)),
            dma((COUNT - 1,)), dma((COUNT - 1,)),
        ],
        compiler_params=pltpu.CompilerParams(
            collective_id=0, has_side_effects=True, vmem_limit_bytes=63 * 2**20
        ),
        cost_estimate=pl.CostEstimate(
            flops=16 * 10**9, bytes_accessed=2 * 10**6, transcendentals=3 * 10**6
        ),
    )(projections, extras)
    return losses[0, :rows], gradient


def solution(mesh):
    return jax.shard_map(
        local,
        mesh=mesh,
        in_specs=(P(("grp", "dev"), None), P(("grp", "dev")), P(("grp", "dev"))),
        out_specs=(P(("grp", "dev")), P(("grp", "dev"), None)),
        check_vma=False,
    )
```

time: 941 us -> 113 us (0.12)
  blocking collectives: 474 us -> 0 us
  waiting for transfers between devices: 317 us -> 0 us
  Pallas kernels: 0 us -> 106 us
  matrix products: 93.8 us -> 0 us
  between operations: 15.8 us -> 0.66 us
  local copies, waits for them, and re-layouts: 19.3 us -> 4.67 us
  loops' own time: 10.9 us -> 0 us
    unnamed x4 -> x0, blocking collectives: 474 us -> none
    reduce_scatter x1 -> x0, waiting for transfers between devices: 273 us -> none  [local(): lax.psum_scatter(lax.map(piece_term, jnp.arange(piece_count, dtype=jnp.in...]
    pallas_call x0 -> x1, Pallas kernels: none -> 106 us  [local(): pl.pallas_call(kernel, out_shape=(jax.ShapeDtypeStruct((8, block), f32),...]
    dot_general x16 -> x0, matrix products: 93.8 us -> none  [the longest x8 64.3 us: piece_term(): jnp.dot(weights_tile, cross_views, preferred_element_type=jnp.float32)]
    all_gather x2 -> x0, waiting for transfers between devices: 42.8 us -> none  [the longest x1 42.7 us: local(): lax.all_gather(views, 'dev', axis=0, tiled=True)]
    dynamic_slice x50 -> x0, local copies, waits for them, and re-layouts: 12.8 us -> none  [the longest x16 9.57 us: local(): lax.map(row_stats, jnp.arange(block_count, dtype=jnp.int32))]
    another operation x2 -> x0, loops' own time: 10.9 us -> none  [the longest x1 5.69 us: local(): lax.map(row_stats, jnp.arange(block_count, dtype=jnp.int32))]
  transfers between devices with their start and end apart: 4 -> 0, of which waited for: 2 -> 0; matrix products, arithmetic and copies ran while one was open for 0% -> 0% of each run, Pallas kernels for 0% -> 0%
where the time goes in v1:
time: 113 us; the launch traced here: 112 us
  Pallas kernels  106 us (94%)
  local copies, waits for them, and re-layouts  4.67 us (4%)
    pallas_call x1, Pallas kernels, local(): pl.pallas_call(kernel, out_shape=(jax.ShapeDtypeStruct((8, block), f32),...  106 us
    unnamed x5, local copies, waits for them, and re-layouts  3.41 us

profile of v1, /device:TPU:0, one launch (start us, length us, event | category | flops | bytes accessed | tf_op | source)
XLA Modules:
  0.0 112.4 jit_solution(11676070914206093076)
XLA Ops:
  0.6 0.0 copy-start.1
  0.7 0.6 copy-done.1
  1.3 0.0 copy-start
  1.3 0.7 copy-done
  2.0 0.7 pad_select_fusion.xw_ref
  2.7 106.4 %shard_map.50 = (f32[8,384]{1,0:T(8,128)}, f32[192,1024]{1,0:T(8,128)}) custom-call(f32[192,1024]{1,0:T(8,128)} %x_ref.1, f32[8,384]{1,0:T(8,128)} %pad_select_fusion.xw_ref), custom_call_target="tpu_custom_call" | custom-call | flops 16000000000 | bytes 2000000 | tf_op jit(solution)/shard_map/pallas_call | solution.py:500
  109.1 1.3 %slice.3 = f32[1,192]{1,0:T(1,128)} slice(f32[8,384]{1,0:T(8,128)} %get-tuple-element.4), slice={[0:1], [0:192]} | slice | bytes 1536 | tf_op jit(solution)/shard_map/slice | solution.py:546
  110.3 2.1 %copy.6 = f32[192,1024]{1,0:T(8,128)} copy(f32[192,1024]{1,0:T(8,128)} %get-tuple-element.9) | data formatting | bytes 1572864
  (3 shorter events, 0.0 us)
Async XLA Ops:
  0.6 0.7 copy-start.1
  1.3 0.7 copy-start

commit v2 on v1

--- a/solution.py
+++ b/solution.py
@@ -18,15 +18,31 @@
 SELF = 10
 COUNT = 11
 STEPS = (
-    ((7, 10, 2, 8, 2), (9, 7, 2, 8, 2), (4, 7, 2, 6, 2), (10, 10, 2, 6, 2), (7, 5, 2, 1, 2),
-     (9, 6, 2, 3, 1), (5, 8, 2, 1, 1), (2, 8, 2, 3, 2), (0, 5, 1, 6, 1)),
-    ((10, 9, 2, 8, 2), (6, 8, 2, 5, 1), (2, 4, 2, 6, 2), (9, 5, 2, 2, 2), (4, 8, 2, 1, 2),
-     (1, 9, 2, 6, 1), (3, 10, 2, 4, 2), (0, 10, 2, 8, 2), (0, 1, 1, 2, 2)),
+    ((10, 10, 2, 7, 2), (8, 9, 2, 5, 2), (9, 7, 2, 5, 2), (2, 5, 2, 4, 2), (3, 10, 2, 8, 2),
+     (6, 8, 2, 5, 1), (8, 2, 2, 1, 2), (1, 9, 2, 4, 2), (0, 2, 2, 1, 1)),
+    ((10, 8, 2, 5, 2), (4, 10, 2, 8, 2), (2, 7, 2, 3, 2), (9, 2, 2, 3, 1), (6, 2, 2, 4, 2),
+     (5, 7, 2, 1, 1), (3, 4, 2, 0, 2), (0, 10, 2, 5, 1), (6, 1, 1, 0, 1)),
 )
 NSTEP = 9
+ROUNDS = (
+    ((9, 0), (7, 0), (8, 0), (5, 0), (9, 1), (7, 1), (8, 1), (5, 1), (9, 2), (7, 2), (8, 2), (5, 2)),
+    (),
+    ((4, 0), (2, 0), (3, 0), (6, 0), (1, 0)),
+    ((4, 1), (2, 1), (3, 1), (6, 1), (1, 1)),
+    ((4, 2), (0, 0), (2, 2), (3, 2), (6, 2), (1, 2)),
+    (),
+    ((0, 1),),
+    (),
+    ((0, 2),),
+    (), (), (), (),
+)
+ROUND_STEP = (
+    (0, 1, 2, -1, 3, 4, 5, 6, 7, 8, -1, -1, -1),
+    (0, -1, -1, -1, 1, 2, 3, 4, 5, 6, 7, 8, -1),
+)
 ZERO = 2 * NSTEP
 CHUNKS = 3
-RB = 32
+RB = 96
 
 NT = (((1,), (1,)), ((), ()))
 NN = (((1,), (0,)), ((), ()))
@@ -42,9 +58,10 @@
 
 
 EDGE = tuple(diff(SLOTS[k], SLOTS[PARENT[k]]) for k in range(COUNT - 1))
-PARTNERS = sorted(
-    {d for s in SLOTS[:SELF] + EDGE for d in (s, neg(s))}
-)
+GREET = tuple(sorted(set(EDGE)))
+
+
+ORDER = (4, 9, 6, 0, 2, 3, 1, 7, 5, 8, 10)
 
 
 def backward_plan():
@@ -52,7 +69,7 @@
     for steps in STEPS:
         prep, rows, cols, cols_a = [], [], [], []
         pb, rb, cb = [0], [0], [0]
-        for k in range(COUNT):
+        for k in ORDER:
             mine = []
             for t, (a, b1, _, b2, _) in enumerate(steps):
                 if k in (a, b1, b2) and t not in prep:
@@ -76,10 +93,17 @@
 PLAN = backward_plan()
 
 UP_AFTER = (
-    (), ((0, 0), (0, 1), (0, 2)), ((1, 0), (1, 1), (1, 2)), ((2, 0), (2, 1), (2, 2)),
-    ((3, 0), (3, 1), (3, 2)), ((4, 0),), ((5, 0), (5, 1), (5, 2), (4, 1)),
-    ((6, 0), (6, 1), (6, 2), (4, 2)), ((7, 0), (8, 0)), ((9, 0), (7, 1), (8, 1)),
-    ((7, 2), (8, 2), (9, 1), (9, 2)),
+    (),
+    (),
+    (),
+    ((6, 0), (6, 1), (6, 2)),
+    ((0, 0), (0, 1), (0, 2)),
+    ((2, 0), (2, 1), (2, 2)),
+    ((3, 0), (4, 0), (3, 1), (3, 2)),
+    ((1, 0), (1, 1), (4, 1), (1, 2)),
+    ((4, 2), (9, 0)),
+    ((7, 0), (9, 1), (5, 0), (5, 1), (5, 2), (7, 1), (8, 0), (8, 1), (8, 2), (9, 2)),
+    ((7, 2),),
 )
 UPS = tuple(e for l in UP_AFTER for e in l)
 UP_BOUND = tuple(sum(len(l) for l in UP_AFTER[:i]) for i in range(COUNT + 1))
@@ -121,7 +145,7 @@
     sibling = device((0, 0, 0), 1 - c)
 
     barrier = pltpu.get_barrier_semaphore()
-    for d in PARTNERS:
+    for d in GREET:
         pl.semaphore_signal(barrier, inc=1, device_id=device(d, c), device_id_type=MESH)
     pl.semaphore_signal(barrier, inc=1, device_id=sibling, device_id_type=MESH)
 
@@ -146,7 +170,7 @@
     for ref in (rsum, rpos, csum, cpos):
         ref[...] = jnp.zeros_like(ref)
 
-    pl.semaphore_wait(barrier, len(PARTNERS) + 1)
+    pl.semaphore_wait(barrier, len(GREET) + 1)
 
     def piece(k, j, core):
         if j == CHUNKS:
@@ -179,53 +203,24 @@
             twin_copy(k, j).wait_recv()
         XB[k] = XT[k, 0] + XT[k, 1]
 
-    for k in (9, 8, 7, 6, 5):
+    for k in (9, 8, 7, 5, 6):
         tree_copy(k, CHUNKS).start()
     for j in range(CHUNKS):
-        for k in (9, 8, 7):
+        for k in (9, 8, 7, 5):
             tree_copy(k, j).start()
-        if j == 0:
-            tree_copy(5, 0).start()
+    for j in range(CHUNKS):
+        tree_copy(6, j).start()
     for j in range(CHUNKS + 1):
         twin_copy(SELF, j).start()
 
-    def gate0():
-        for k in (9, 8, 7):
-            arrive(k, CHUNKS)
-        for j in range(CHUNKS):
-            arrive(9, j)
-            if j + 1 < CHUNKS:
-                tree_copy(5, j + 1).start()
-            arrive(8, j)
-            arrive(7, j)
-            tree_copy(6, j).start()
-        for k in (SELF, 9, 8, 7):
-            twins(k)
-
-    def gate1():
-        for k in (5, 6, 4):
-            arrive(k, CHUNKS)
-        for j in range(CHUNKS):
-            arrive(4, j)
-            arrive(5, j)
-        for j in range(CHUNKS):
-            arrive(6, j)
-        for k in (5, 4, 6):
-            twins(k)
-
-    def gate2():
-        for k in (3, 2, 1):
-            arrive(k, CHUNKS)
-        for j in range(CHUNKS):
-            for k in (3, 2, 1):
-                arrive(k, j)
-        for k in (3, 2, 1):
-            twins(k)
-
-    def gate3():
-        for j in (CHUNKS,) + tuple(range(CHUNKS)):
-            arrive(0, j)
-        twins(0)
+    def gate(events):
+        for k, j in events:
+            if j == 0:
+                arrive(k, CHUNKS)
+            arrive(k, j)
+        for k, j in events:
+            if j == CHUNKS - 1:
+                twins(k)
 
     def step_of(t):
         cols = [[[s[n] for s in STEPS[core]] for n in range(5)] for core in (0, 1)]
@@ -251,30 +246,40 @@
     def column_ids(b):
         return (base_of(b) + lane + jnp.where(lane >= rows, far, 0)).astype(jnp.float32)
 
-    def score_step(t, _):
-        for n, gate in ((0, gate0), (1, gate1), (2, gate2), (7, gate3)):
-            pl.when(t == n)(gate)
+    def score_round(n, _):
+        for m, events in enumerate(ROUNDS):
+            if events:
+                @pl.when(n == m)
+                def _(events=events):
+                    gate(events)
+                    if events == ROUNDS[0]:
+                        twins(SELF)
+        t = lut2(n, c, ROUND_STEP[0], ROUND_STEP[1])
+        pl.when(t >= 0)(lambda: score_step(t))
+        return 0
+
+    def score_step(t):
         a, b1, b2, partner, weight = tile_rows(t)
         S[...] = lax.dot_general(
             V[a], jnp.concatenate([V[b1], V[b2]], axis=0), NT, preferred_element_type=jnp.float32
         )
         ids = jnp.concatenate([column_ids(b1), column_ids(b2)], axis=1)
 
+        offset = inv_temp - jnp.log(weight)
+        half1, half2 = weight[0:1, 0:128], weight[0:1, block : block + 128]
+
         def rows_body(i, carry):
             es, ps_ = carry
             r = pl.multiple_of(i * RB, RB)
-            s = S[pl.ds(r, RB), :] * inv_temp
+            s = S[pl.ds(r, RB), :]
             rid = row_ids(a, r)
-            e = jnp.exp(s - inv_temp) * weight
-            e = jnp.where(rid == ids, 0.0, e)
-            m = jnp.where(rid == partner, s * weight, 0.0)
+            e = jnp.where(rid == ids, 0.0, jnp.exp(s * inv_temp - offset))
+            m = jnp.where(rid == partner, s, 0.0)
             E[t, pl.ds(r, RB), :] = e
-            er, mr_ = e[:, :128], m[:, :128]
-            for n in range(1, 2 * block // 128):
-                er = er + e[:, n * 128 : (n + 1) * 128]
-                mr_ = mr_ + m[:, n * 128 : (n + 1) * 128]
-            rsum[a, pl.ds(r, RB), :] += er
-            rpos[a, pl.ds(r, RB), :] += mr_
+            er = [e[:, n * 128 : (n + 1) * 128] for n in range(6)]
+            mr_ = [m[:, n * 128 : (n + 1) * 128] for n in range(6)]
+            rsum[a, pl.ds(r, RB), :] += er[0] + er[1] + er[2] + er[3] + er[4] + er[5]
+            rpos[a, pl.ds(r, RB), :] += (mr_[0] + mr_[1] + mr_[2]) * half1 + (mr_[3] + mr_[4] + mr_[5]) * half2
             for n in range(RB // 8):
                 es = es + e[n * 8 : (n + 1) * 8, :]
                 ps_ = ps_ + m[n * 8 : (n + 1) * 8, :]
@@ -282,44 +287,25 @@
 
         zero = jnp.zeros((8, 2 * block), jnp.float32)
         es, ps_ = lax.fori_loop(0, block // RB, rows_body, (zero, zero))
+        ps_ = ps_ * weight
         for n, b in ((0, b1), (1, b2)):
             use = jnp.where(a == b, 0.0, 1.0)
             csum[b] += es[:, n * block : (n + 1) * block] * use
             cpos[b] += ps_[:, n * block : (n + 1) * block] * use
-        return 0
-
-    lax.fori_loop(0, NSTEP, score_step, 0)
+
+    lax.fori_loop(0, 12, score_round, 0)
 
     def total(rs, cs):
         return jnp.sum(rs.T, axis=0, keepdims=True) + jnp.sum(cs, axis=0, keepdims=True)
 
-    def sums_body(k, _):
-        SO[k, 0:1, :] = total(rsum[k], csum[k])
-        SO[k, 1:2, :] = total(rpos[k], cpos[k])
-        return 0
-
-    SO[...] = jnp.zeros_like(SO)
-    lax.fori_loop(0, COUNT, sums_body, 0)
-
-    twin_sums = pltpu.make_async_remote_copy(
-        src_ref=SO, dst_ref=SI, send_sem=ms, recv_sem=mr, device_id=sibling, device_id_type=MESH
-    )
-    twin_sums.start()
-
-    def wide(row):
-        return jnp.broadcast_to(row, (128, block)).T
-
-    def wcol_body(k, _):
-        wcol[k] = wide(XB[k, 0:1, :])
-        return 0
-
-    lax.fori_loop(0, COUNT, wcol_body, 0)
-    twin_sums.wait()
-    SI[...] = SO[...] + SI[...]
+    def sums_of(k):
+        SO[k] = jnp.concatenate(
+            [total(rsum[k], csum[k]), total(rpos[k], cpos[k]), jnp.zeros((6, block), jnp.float32)], axis=0
+        )
 
     def sum_copy(k):
         return pltpu.make_async_remote_copy(
-            src_ref=SI.at[k], dst_ref=SR.at[k], send_sem=ps.at[k], recv_sem=pr.at[k],
+            src_ref=SO.at[k], dst_ref=SR.at[k], send_sem=ps.at[k], recv_sem=pr.at[k],
             device_id=device(SLOTS[k], c), device_id_type=MESH,
         )
 
@@ -330,28 +316,41 @@
         )
 
     for k in range(COUNT - 1):
+        sums_of(k)
         sum_copy(k).start()
-    both = SI[SELF]
+    sums_of(SELF)
+
+    def wide(row):
+        return jnp.broadcast_to(row, (128, block)).T
+
+    def wcol_body(k, _):
+        wcol[k] = wide(XB[k, 0:1, :])
+        return 0
+
+    lax.fori_loop(0, COUNT, wcol_body, 0)
+    C[ZERO] = jnp.zeros((block, block), jnp.bfloat16)
+    acc[...] = jnp.zeros_like(acc)
+    mine = SO[SELF]
     for k in range(COUNT - 1):
         sum_copy(k).wait_recv()
-        both = both + SR[k]
-    exp_sum, positive = both[0:1, :], both[1:2, :]
+        mine = mine + SR[k]
+    SI[0] = mine
+    twin_sums = pltpu.make_async_remote_copy(
+        src_ref=SI.at[0], dst_ref=SI.at[1], send_sem=ms, recv_sem=mr, device_id=sibling, device_id_type=MESH
+    )
+    twin_sums.start()
+    twin_sums.wait()
+    both = SI[0] + SI[1]
+    exp_sum, positive = both[0:1, :], both[1:2, :] * inv_temp
     scale = XB[SELF, 0:1, :] / exp_sum
     AO[...] = jnp.broadcast_to(scale, (8, block))
     for k in range(COUNT - 1):
         scale_copy(k).start()
     AR[SELF] = AO[...]
     losses = jnp.broadcast_to(inv_temp + jnp.log(exp_sum) - positive, (8, block))
-    loss_ref[...] = jnp.where(c == 0, losses, pltpu.roll(losses, rows, 1))
-    C[ZERO] = jnp.zeros((block, block), jnp.bfloat16)
+    loss_ref[...] = jnp.where(c == 0, losses, pltpu.roll(losses, rows, 1))[0:1, :rows]
     for k in range(COUNT - 1):
         scale_copy(k).wait_recv()
-
-    def acol_body(k, _):
-        acol[k] = wide(AR[k, 0:1, :])
-        return 0
-
-    lax.fori_loop(0, COUNT, acol_body, 0)
 
     def twin_part(k):
         return pltpu.make_async_remote_copy(
@@ -398,13 +397,14 @@
     def prepare(n, _):
         t = lut2(n, c, PLAN[0][0], PLAN[1][0])
         a, b1, b2, partner, weight = tile_rows(t)
+        acol[...] = wide(AR[a, 0:1, :])
         arow = jnp.concatenate([AR[b1, 0:1, :], AR[b2, 0:1, :]], axis=1)
         wrow = jnp.concatenate([XB[b1, 0:1, :], XB[b2, 0:1, :]], axis=1)
 
         def rows_body(i, _):
             r = pl.multiple_of(i * RB, RB)
             rid = row_ids(a, r)
-            ac, wc = acol[a, pl.ds(r, RB), :], wcol[a, pl.ds(r, RB), :]
+            ac, wc = acol[pl.ds(r, RB), :], wcol[a, pl.ds(r, RB), :]
             ac = jnp.concatenate([ac] * (2 * block // 128), axis=1)
             wc = jnp.concatenate([wc] * (2 * block // 128), axis=1)
             v = E[t, pl.ds(r, RB), :] * (ac + arow)
@@ -437,17 +437,27 @@
         )
         return 0
 
-    def slot_body(k, _):
+    def slot_body(i, _):
+        k = lut(i, ORDER)
         for n, body in ((3, prepare), (4, row_product), (5, column_product)):
-            if n == 4:
-                acc[...] = jnp.zeros_like(acc)
-            lo = lut2(k, c, PLAN[0][n][:-1], PLAN[1][n][:-1])
-            hi = lut2(k, c, PLAN[0][n][1:], PLAN[1][n][1:])
+            lo = lut2(i, c, PLAN[0][n][:-1], PLAN[1][n][:-1])
+            hi = lut2(i, c, PLAN[0][n][1:], PLAN[1][n][1:])
             lax.fori_loop(lo, hi, body, 0)
-        H[k] = acc[pl.ds(own, rows), :]
-        TX[k] = acc[pl.ds(other, rows), :].astype(jnp.bfloat16)
+
+        def split(n, _):
+            r = pl.multiple_of(n * 32, 32)
+            theirs = pl.ds(pl.multiple_of(other + r, 32), 32)
+            ours = pl.ds(pl.multiple_of(own + r, 32), 32)
+            TX[k, pl.ds(r, 32), :] = acc[theirs, :].astype(jnp.bfloat16)
+            H[k, pl.ds(r, 32), :] = acc[ours, :]
+            zero = jnp.zeros((32, width), jnp.float32)
+            acc[theirs, :] = zero
+            acc[ours, :] = zero
+            return 0
+
+        lax.fori_loop(0, rows // 32, split, 0)
         twin_part(k).start()
-        lax.fori_loop(lut(k, UP_BOUND[:-1]), lut(k, UP_BOUND[1:]), up_event, 0)
+        lax.fori_loop(lut(i, UP_BOUND[:-1]), lut(i, UP_BOUND[1:]), up_event, 0)
         return 0
 
     lax.fori_loop(0, COUNT, slot_body, 0)
@@ -500,7 +510,7 @@
     losses, gradient = pl.pallas_call(
         kernel,
         out_shape=(
-            jax.ShapeDtypeStruct((8, block), f32),
+            jax.ShapeDtypeStruct((1, rows), f32),
             jax.ShapeDtypeStruct((rows, width), f32),
         ),
         in_specs=[pl.BlockSpec(memory_space=vm)] * 2,
@@ -522,11 +532,11 @@
             vm((COUNT, 8, block), f32),
             vm((COUNT, 8, block), f32),
             vm((COUNT, 8, block), f32),
-            vm((COUNT, 8, block), f32),
+            vm((2, 8, block), f32),
             vm((COUNT - 1, 8, block), f32),
             vm((8, block), f32),
             vm((COUNT, 8, block), f32),
-            vm((COUNT, block, 128), f32),
+            vm((block, 128), f32),
             vm((COUNT, block, 128), f32),
             dma((COUNT - 1, CHUNKS + 1)), dma((COUNT - 1, CHUNKS + 1)),
             dma((COUNT, CHUNKS + 1)), dma((COUNT, CHUNKS + 1)),
@@ -543,7 +553,7 @@
             flops=16 * 10**9, bytes_accessed=2 * 10**6, transcendentals=3 * 10**6
         ),
     )(projections, extras)
-    return losses[0, :rows], gradient
+    return losses.reshape(rows), gradient
 
 
 def solution(mesh):

time: 113 us -> 104 us (0.920)
  Pallas kernels: 106 us -> 98.3 us
    pallas_call x1, Pallas kernels: 106 us -> 98.3 us  [local(): pl.pallas_call(kernel, out_shape=(jax.ShapeDtypeStruct((1, rows), f32), j...]
    slice x1 -> x0, local copies, waits for them, and re-layouts: 1.26 us -> none  [local(): return (losses[0, :rows], gradient)]
    unnamed x5 -> x8, local copies, waits for them, and re-layouts: 3.41 us -> 4.6 us
where the time goes in v2:
time: 104 us
  Pallas kernels  98.3 us (95%)
  local copies, waits for them, and re-layouts  4.6 us (4%)
    pallas_call x1, Pallas kernels, local(): pl.pallas_call(kernel, out_shape=(jax.ShapeDtypeStruct((1, rows), f32), j...  98.3 us
    unnamed x8, local copies, waits for them, and re-layouts  4.6 us

profile of v2, /device:TPU:0, one launch (start us, length us, event | category | flops | bytes accessed | tf_op | source)
XLA Modules:
  0.0 104.3 jit_solution(6469829187394566792)
XLA Ops:
  0.6 0.0 copy-start.2
  0.7 0.6 copy-done.2
  1.3 0.0 copy-start
  1.3 0.7 copy-done
  2.0 0.7 pad_select_fusion.xw_ref
  2.7 98.3 %shard_map.50 = (f32[1,192]{1,0:T(1,128)}, f32[192,1024]{1,0:T(8,128)}) custom-call(f32[192,1024]{1,0:T(8,128)} %x_ref.1, f32[8,384]{1,0:T(8,128)} %pad_select_fusion.xw_ref), custom_call_target="tpu_custom_call" | custom-call | flops 16000000000 | bytes 2000000 | tf_op jit(solution)/shard_map/pallas_call | solution.py:510
  101.0 0.0 copy-start.1
  101.0 0.6 copy-done.1
  101.6 0.6 copy.7
  102.2 2.1 %copy.8 = f32[192,1024]{1,0:T(8,128)} copy(f32[192,1024]{1,0:T(8,128)} %get-tuple-element.9) | data formatting | bytes 1572864
  (3 shorter events, 0.0 us)
Async XLA Ops:
  0.6 0.7 copy-start.2
  1.3 0.7 copy-start
  101.0 0.6 copy-start.1

commit v3 on v2

--- a/solution.py
+++ b/solution.py
@@ -42,6 +42,7 @@
 )
 ZERO = 2 * NSTEP
 CHUNKS = 3
+PB = 96
 RB = 96
 
 NT = (((1,), (1,)), ((), ()))
@@ -109,24 +110,40 @@
 UP_BOUND = tuple(sum(len(l) for l in UP_AFTER[:i]) for i in range(COUNT + 1))
 
 
+def words(table):
+    out = []
+    for n in range(0, len(table), 8):
+        w = sum(v << (4 * m) for m, v in enumerate(table[n : n + 8]))
+        out.append(w - 2**32 if w >= 2**31 else w)
+    return out
+
+
 def lut(i, table):
-    v = jnp.int32(table[0])
-    for n in range(1, len(table)):
-        v = jnp.where(i == n, jnp.int32(table[n]), v)
-    return v
+    if max(table) > 15:
+        return lut(i, [v % 16 for v in table]) + 16 * lut(i, [v // 16 for v in table])
+    return pick(i, [jnp.int32(w) for w in words(table)])
 
 
 def lut2(i, c, t0, t1):
     n = max(len(t0), len(t1))
     t0 = tuple(t0) + (0,) * (n - len(t0))
     t1 = tuple(t1) + (0,) * (n - len(t1))
-    if t0 == t1:
-        return lut(i, t0)
-    return lut(i, t0) * (1 - c) + lut(i, t1) * c
+    if max(t0 + t1) > 15:
+        low, high = ([[v % 16 for v in t] for t in (t0, t1)], [[v // 16 for v in t] for t in (t0, t1)])
+        return lut2(i, c, *low) + 16 * lut2(i, c, *high)
+    return pick(i, [jnp.where(c == 0, jnp.int32(a), jnp.int32(b)) for a, b in zip(words(t0), words(t1))])
+
+
+def pick(i, ws):
+    i = jnp.asarray(i, jnp.int32)
+    v = ws[0]
+    for n in range(1, len(ws)):
+        v = jnp.where(i >= 8 * n, ws[n], v)
+    return (v >> ((i % 8) * 4)) % 16
 
 
 def kernel(
-    x_ref, xw_ref, loss_ref, grad_ref,
+    x_ref, w_ref, partner_ref, loss_ref, grad_ref,
     V, XT, XB, E, C, S, acc, H, TX, RX, RC, rsum, rpos, csum, cpos, SO, SI, SR, AO, AR, acol, wcol,
     gs, gr, ss, sr, us, ur, ts, tr, ms, mr, ps, pr, qs, qr,
 ):
@@ -166,7 +183,11 @@
         return 0
 
     lax.fori_loop(0, rows // 32, norm_body, 0)
-    XT[SELF, c] = xw_ref[...]
+    AO[...] = jnp.zeros_like(AO)
+    AO[0:1, 0:rows] = w_ref[...].astype(jnp.float32)
+    AO[1:2, 0:rows] = partner_ref[...].astype(jnp.float32)
+    extras = AO[...]
+    XT[SELF, c] = jnp.where(c == 0, extras, pltpu.roll(extras, rows, 1))
     for ref in (rsum, rpos, csum, cpos):
         ref[...] = jnp.zeros_like(ref)
 
@@ -239,8 +260,8 @@
         )
         return a, b1, b2, partner, weight
 
-    def row_ids(a, r):
-        start = base_of(a) + r + jnp.where(r >= rows, far, 0)
+    def row_ids(base, r):
+        start = base + r + jnp.where(r >= rows, far, 0)
         return (start + sub_row).astype(jnp.float32)
 
     def column_ids(b):
@@ -254,7 +275,7 @@
                     gate(events)
                     if events == ROUNDS[0]:
                         twins(SELF)
-        t = lut2(n, c, ROUND_STEP[0], ROUND_STEP[1])
+        t = lut2(n, c, [v + 1 for v in ROUND_STEP[0]], [v + 1 for v in ROUND_STEP[1]]) - 1
         pl.when(t >= 0)(lambda: score_step(t))
         return 0
 
@@ -263,6 +284,7 @@
         S[...] = lax.dot_general(
             V[a], jnp.concatenate([V[b1], V[b2]], axis=0), NT, preferred_element_type=jnp.float32
         )
+        base = base_of(a)
         ids = jnp.concatenate([column_ids(b1), column_ids(b2)], axis=1)
 
         offset = inv_temp - jnp.log(weight)
@@ -272,7 +294,7 @@
             es, ps_ = carry
             r = pl.multiple_of(i * RB, RB)
             s = S[pl.ds(r, RB), :]
-            rid = row_ids(a, r)
+            rid = row_ids(base, r)
             e = jnp.where(rid == ids, 0.0, jnp.exp(s * inv_temp - offset))
             m = jnp.where(rid == partner, s, 0.0)
             E[t, pl.ds(r, RB), :] = e
@@ -397,23 +419,24 @@
     def prepare(n, _):
         t = lut2(n, c, PLAN[0][0], PLAN[1][0])
         a, b1, b2, partner, weight = tile_rows(t)
+        base = base_of(a)
         acol[...] = wide(AR[a, 0:1, :])
         arow = jnp.concatenate([AR[b1, 0:1, :], AR[b2, 0:1, :]], axis=1)
         wrow = jnp.concatenate([XB[b1, 0:1, :], XB[b2, 0:1, :]], axis=1)
 
         def rows_body(i, _):
-            r = pl.multiple_of(i * RB, RB)
-            rid = row_ids(a, r)
-            ac, wc = acol[pl.ds(r, RB), :], wcol[a, pl.ds(r, RB), :]
+            r = pl.multiple_of(i * PB, PB)
+            rid = row_ids(base, r)[:PB]
+            ac, wc = acol[pl.ds(r, PB), :], wcol[a, pl.ds(r, PB), :]
             ac = jnp.concatenate([ac] * (2 * block // 128), axis=1)
             wc = jnp.concatenate([wc] * (2 * block // 128), axis=1)
-            v = E[t, pl.ds(r, RB), :] * (ac + arow)
+            v = E[t, pl.ds(r, PB), :] * (ac + arow)
             v = (v - jnp.where(rid == partner, (wc + wrow) * weight, 0.0)).astype(jnp.bfloat16)
-            C[2 * t, pl.ds(r, RB), :] = v[:, :block]
-            C[2 * t + 1, pl.ds(r, RB), :] = v[:, block:]
+            C[2 * t, pl.ds(r, PB), :] = v[:, :block]
+            C[2 * t + 1, pl.ds(r, PB), :] = v[:, block:]
             return 0
 
-        lax.fori_loop(0, block // RB, rows_body, 0)
+        lax.fori_loop(0, block // PB, rows_body, 0)
         return 0
 
     def row_product(n, _):
@@ -457,7 +480,9 @@
 
         lax.fori_loop(0, rows // 32, split, 0)
         twin_part(k).start()
-        lax.fori_loop(lut(i, UP_BOUND[:-1]), lut(i, UP_BOUND[1:]), up_event, 0)
+        first = lut(i, UP_BOUND[:-1])
+        count = lut(i, [len(u) for u in UP_AFTER])
+        lax.fori_loop(first, first + count, up_event, 0)
         return 0
 
     lax.fori_loop(0, COUNT, slot_body, 0)
@@ -498,13 +523,6 @@
 def local(projections, row_weights, partner):
     rows, width = projections.shape
     block = 2 * rows
-    core = lax.axis_index("grp") % 2
-    mine = jnp.stack([row_weights.astype(jnp.float32), partner.astype(jnp.float32)])
-    mine = jnp.pad(mine, ((0, 6), (0, 0)))
-    none = jnp.zeros_like(mine)
-    extras = jnp.where(
-        core == 0, jnp.concatenate([mine, none], 1), jnp.concatenate([none, mine], 1)
-    )
     f32, bf16 = jnp.float32, jnp.bfloat16
     vm, dma = pltpu.VMEM, pltpu.SemaphoreType.DMA
     losses, gradient = pl.pallas_call(
@@ -513,7 +531,7 @@
             jax.ShapeDtypeStruct((1, rows), f32),
             jax.ShapeDtypeStruct((rows, width), f32),
         ),
-        in_specs=[pl.BlockSpec(memory_space=vm)] * 2,
+        in_specs=[pl.BlockSpec(memory_space=vm)] * 3,
         out_specs=[pl.BlockSpec(memory_space=vm)] * 2,
         scratch_shapes=[
             vm((COUNT, block, width), bf16),
@@ -552,7 +570,7 @@
         cost_estimate=pl.CostEstimate(
             flops=16 * 10**9, bytes_accessed=2 * 10**6, transcendentals=3 * 10**6
         ),
-    )(projections, extras)
+    )(projections, row_weights.reshape(1, rows), partner.reshape(1, rows))
     return losses.reshape(rows), gradient
 
 

time: 104 us -> 103 us (level)
  Pallas kernels: 98.3 us -> 97.2 us
    pallas_call x1, Pallas kernels: 98.3 us -> 97.2 us  [local(): pl.pallas_call(kernel, out_shape=(jax.ShapeDtypeStruct((1, rows), f32), j...]
    unnamed x8 -> x6, local copies, waits for them, and re-layouts: 4.6 us -> 3.96 us
where the time goes in v3:
time: 103 us; the launch traced here: 102 us
  Pallas kernels  97.2 us (94%)
  local copies, waits for them, and re-layouts  4.52 us (4%)
    pallas_call x1, Pallas kernels, local(): pl.pallas_call(kernel, out_shape=(jax.ShapeDtypeStruct((1, rows), f32), j...  97.2 us
    unnamed x6, local copies, waits for them, and re-layouts  3.96 us

profile of v3, /device:TPU:0, one launch (start us, length us, event | category | flops | bytes accessed | tf_op | source)
XLA Modules:
  0.0 102.4 jit_solution(241428487525575601)
XLA Ops:
  0.6 0.0 copy-start.1
  0.6 0.6 copy-done.1
  1.3 0.6 reshape.13.w_ref
  1.9 97.2 %shard_map.50 = (f32[1,192]{1,0:T(1,128)}, f32[192,1024]{1,0:T(8,128)}) custom-call(f32[192,1024]{1,0:T(8,128)} %x_ref.1, bf16[1,192]{1,0:T(2,128)(2,1)} %reshape.13.w_ref, s32[1,192]{1,0:T(1,128)} %bitcast.3), custom_call_target="tpu_custom_call" | custom-call | flops 16000000000 | bytes 2000000 | tf_op jit(solution)/shard_map/pallas_call | solution.py:528
  99.1 0.0 copy-start
  99.1 0.7 copy-done
  99.7 0.6 copy.7
  100.3 2.1 %copy.8 = f32[192,1024]{1,0:T(8,128)} copy(f32[192,1024]{1,0:T(8,128)} %get-tuple-element.9) | data formatting | bytes 1572864
Async XLA Ops:
  0.6 0.7 copy-start.1
  99.1 0.7 copy-start

commit v4 on v3

--- a/solution.py
+++ b/solution.py
@@ -371,6 +371,13 @@
     AR[SELF] = AO[...]
     losses = jnp.broadcast_to(inv_temp + jnp.log(exp_sum) - positive, (8, block))
     loss_ref[...] = jnp.where(c == 0, losses, pltpu.roll(losses, rows, 1))[0:1, :rows]
+    for k in range(COUNT):
+        for j in range(CHUNKS + 1):
+            if k < SELF:
+                tree_copy(k, j).wait_send()
+            twin_copy(k, j).wait_send()
+    for k in range(COUNT - 1):
+        sum_copy(k).wait_send()
     for k in range(COUNT - 1):
         scale_copy(k).wait_recv()
 
@@ -509,15 +516,9 @@
     lax.fori_loop(0, CHUNKS, finish, 0)
 
     for k in range(COUNT - 1):
-        for j in range(CHUNKS + 1):
-            tree_copy(k, j).wait_send()
         for j in range(CHUNKS):
             up_copy(k, j, EDGE[k]).wait_send()
-        sum_copy(k).wait_send()
         scale_copy(k).wait_send()
-    for k in range(COUNT):
-        for j in range(CHUNKS + 1):
-            twin_copy(k, j).wait_send()
 
 
 def local(projections, row_weights, partner):

time: 103 us -> 102 us (level)
  no operation moved by 1% of the time
where the time goes in v4:
time: 102 us
  Pallas kernels  97.1 us (95%)
  local copies, waits for them, and re-layouts  4.52 us (4%)
    pallas_call x1, Pallas kernels, local(): pl.pallas_call(kernel, out_shape=(jax.ShapeDtypeStruct((1, rows), f32), j...  97.1 us
    unnamed x6, local copies, waits for them, and re-layouts  3.96 us

profile of v4, /device:TPU:0, one launch (start us, length us, event | category | flops | bytes accessed | tf_op | source)
XLA Modules:
  0.0 102.3 jit_solution(6765978542820988620)
XLA Ops:
  0.6 0.0 copy-start.1
  0.6 0.6 copy-done.1
  1.3 0.6 reshape.13.w_ref
  1.9 97.1 %shard_map.50 = (f32[1,192]{1,0:T(1,128)}, f32[192,1024]{1,0:T(8,128)}) custom-call(f32[192,1024]{1,0:T(8,128)} %x_ref.1, bf16[1,192]{1,0:T(2,128)(2,1)} %reshape.13.w_ref, s32[1,192]{1,0:T(1,128)} %bitcast.3), custom_call_target="tpu_custom_call" | custom-call | flops 16000000000 | bytes 2000000 | tf_op jit(solution)/shard_map/pallas_call | solution.py:529
  98.9 0.0 copy-start
  98.9 0.7 copy-done
  99.6 0.6 copy.7
  100.2 2.1 %copy.8 = f32[192,1024]{1,0:T(8,128)} copy(f32[192,1024]{1,0:T(8,128)} %get-tuple-element.9) | data formatting | bytes 1572864
Async XLA Ops:
  0.6 0.7 copy-start.1
  98.9 0.7 copy-start
